TPU v7x, 128 devices: a whole 4x4x4 slice. The times are simulated.
128 devices in a mesh: row: 8 (over y, core), col: 16 (over z, x).
Axes of the slice: x: 4, y: 4, z: 4, core: 2. Of those that a mesh axis runs over, the one named last changes fastest.
Arguments:
- sigma_top: float32 [6144, 6144], P('row', 'col')
- factor_cross: float32 [6144, 6144], P('row', 'col'), may hold values from -0.078125 to 0.078125
- factor_inverse: float32 [6144, 6144], P('row', 'col')
- block_inverse: float32 [6144, 6144], P('row', 'col')
- ancestors: int32 [12], replicated, may hold values from 0 to 23, as said below
Outputs:
- sigma_cross: float32 [6144, 6144], P('row', 'col')
- sigma_child: float32 [6144, 6144], P('row', 'col')
Inputs may be any that keep to these rules, and one draw needn't show every extreme that they name: `ancestors`: 12 distinct block numbers; block 0 and block 23 are always among them.
All inputs are finite; a program needn't handle non-finite values.
Results may differ from a plain program's by a relative error of at most 0.000078.
Values sent between devices are 32-bit elements; how exact they have to be, the bound alone decides.
No kernel may reach another device: no remote copies, remote signals or barrier semaphores. Data moves between devices by JAX's collectives and lax.ppermute only.
A program may use at most 128 MiB of HBM per device.

v0:
```python
import jax
import jax.numpy as jnp
from jax import lax
from jax.sharding import PartitionSpec as P

BLK = 256


def transposed_rows(gathered, right_side):
    return lax.dot_general(
        gathered,
        right_side,
        (((0,), (0,)), ((), ())),
        precision=lax.Precision.HIGHEST,
        preferred_element_type=jnp.float32,
    )


def per_device(sigma_top, factor_cross, factor_inverse, block_inverse, ancestors):
    height = sigma_top.shape[0]
    first_row = lax.axis_index("row") * height
    blocks = (first_row + lax.iota(jnp.int32, height)) // BLK
    living = jnp.any(blocks[:, None] == ancestors[None, :], axis=1)
    masked = jnp.where(living[:, None], factor_cross, jnp.float32(0.0))
    inverse_strip = lax.all_gather(factor_inverse, "row", axis=0, tiled=True)
    rows_used = inverse_strip
    update = jnp.dot(
        lax.all_gather(masked, "col", axis=1, tiled=True),
        rows_used,
        precision=lax.Precision.HIGHEST,
        preferred_element_type=jnp.float32,
    )
    update_strip = lax.all_gather(update, "row", axis=0, tiled=True)
    rows_used = update_strip
    product = jnp.dot(
        lax.all_gather(sigma_top, "col", axis=1, tiled=True),
        rows_used,
        precision=lax.Precision.HIGHEST,
        preferred_element_type=jnp.float32,
    )
    sigma_cross = jnp.where(living[:, None], -product, jnp.float32(0.0))
    gathered = lax.all_gather(sigma_cross, "col", axis=1, tiled=True)
    correction = lax.psum_scatter(
        transposed_rows(gathered, update), "row", scatter_dimension=0, tiled=True
    )
    sigma_child = block_inverse - correction
    return (sigma_cross, sigma_child)


def solution(mesh):
    return jax.shard_map(
        per_device,
        mesh=mesh,
        in_specs=(P("row", "col"), P("row", "col"), P("row", "col"), P("row", "col"), P()),
        out_specs=(P("row", "col"), P("row", "col")),
        check_vma=False,
    )
```

profile of v0, /device:TPU:1, one launch (start us, length us, event | category | flops | bytes accessed | tf_op | source)
XLA Modules:
  0.0 643.4 jit_solution(8413906918570889155)
XLA Ops:
  7.2 0.0 all-gather.8.cloned.1.call-start
  7.2 0.7 all-gather.8.cloned.1.call-update
  7.9 0.0 all-gather.6.cloned.1.call-start
  8.0 0.7 compare_reduce_fusion
  8.7 2.5 broadcast_select_fusion
  11.2 0.0 all-gather.6.cloned.1.call-update
  11.2 0.0 all-gather.12.cloned.1.call-start
  11.2 0.7 all-gather.12.cloned.1.call-update
  11.9 0.0 all-gather.10.cloned.1.call-start
  12.0 55.5 %all-gather.8.cloned.1.call-done = f32[6144,384]{1,0:T(8,128)} async-done(((f32[768,384]{1,0:T(8,128)}), f32[6144,384]{1,0:T(8,128)}) %all-gather.8.cloned.1.call-update) | async-done | bytes 9437200 | tf_op jit(solution)/shard_map/all_gather | solution.py:25
  67.5 124.8 %all-gather.6.cloned.1.call-done = f32[768,6144]{1,0:T(8,128)} async-done(((f32[768,384]{1,0:T(8,128)}), f32[768,6144]{1,0:T(8,128)}) %all-gather.6.cloned.1.call-update) | async-done | bytes 18874384 | tf_op jit(solution)/shard_map/all_gather | solution.py:28
  192.3 34.1 %fusion.5 = f32[768,384]{1,0:T(8,128)} fusion(f32[768,6144]{1,0:T(8,128)} %all-gather.6.cloned.1.call-done, f32[6144,384]{1,0:T(8,128)} %all-gather.8.cloned.1.call-done), kind=kOutput, calls=%fused_computation.14 | convolution fusion | flops 21743271936 | bytes 29491200 | tf_op jit(solution)/shard_map/dot_general | solution.py:27
  226.4 0.0 all-gather.10.cloned.1.call-update
  226.4 0.0 copy-start
  226.4 0.2 all-gather.14.cloned.1.call-start
  226.6 89.7 %all-gather.12.cloned.1.call-done = f32[768,6144]{1,0:T(8,128)} async-done(((f32[768,384]{1,0:T(8,128)}), f32[768,6144]{1,0:T(8,128)}) %all-gather.12.cloned.1.call-update) | async-done | bytes 18874384 | tf_op jit(solution)/shard_map/all_gather | solution.py:36
  316.3 56.3 %all-gather.10.cloned.1.call-done = f32[6144,384]{1,0:T(8,128)} async-done(((f32[768,384]{1,0:T(8,128)}), f32[6144,384]{1,0:T(8,128)}) %all-gather.10.cloned.1.call-update) | async-done | bytes 9437200 | tf_op jit(solution)/shard_map/all_gather | solution.py:33
  372.6 48.7 %fusion.1 = f32[768,384]{0,1:T(8,128)} fusion(f32[6144,384]{1,0:T(8,128)} %all-gather.10.cloned.1.call-done, f32[768,6144]{1,0:T(8,128)} %all-gather.12.cloned.1.call-done, pred[768]{0:T(1024)(128)(4,1)S(1)} %compare_reduce_fusion), kind=kOutput, calls=%fused_computation.2 | convolution fusion | flops 21743861760 | bytes 29491968 | tf_op jit(solution)/shard_map/dot_general | solution.py:35
  421.3 0.0 all-gather.14.cloned.1.call-update
  421.3 0.3 reduce-scatter.2.cloned.1.call-start
  421.6 121.8 %all-gather.14.cloned.1.call-done = f32[768,6144]{0,1:T(8,128)} async-done(((f32[768,384]{0,1:T(8,128)}), f32[768,6144]{0,1:T(8,128)}) %all-gather.14.cloned.1.call-update) | async-done | bytes 18874384 | tf_op jit(solution)/shard_map/all_gather | solution.py:42
  543.4 0.0 copy-done
  543.4 34.0 %fusion.6 = f32[6144,384]{1,0:T(8,128)} fusion(f32[768,6144]{0,1:T(8,128)} %all-gather.14.cloned.1.call-done, f32[768,384]{1,0:T(8,128)S(1)} %copy-done), kind=kOutput, calls=%fused_computation.15 | convolution fusion | flops 21743271936 | bytes 29491200 | tf_op jit(solution)/shard_map/dot_general | solution.py:10
  577.5 0.0 copy-start.1
  577.5 0.0 copy-start.2
  577.5 0.0 reduce-scatter.2.cloned.1.call-update
  577.5 1.2 copy-done.1
  578.8 1.4 copy.8
  580.2 54.0 %reduce-scatter.2.cloned.1.call-done = f32[768,384]{1,0:T(8,128)} async-done(((f32[6144,384]{1,0:T(8,128)}), f32[768,384]{1,0:T(8,128)}) %reduce-scatter.2.cloned.1.call-update) | async-done | bytes 1179664 | tf_op jit(solution)/shard_map/reduce_scatter | solution.py:43
  634.2 0.0 copy-done.2
  634.2 2.4 sub.10
  (1 shorter events, 0.0 us)
Async XLA Ops:
  7.2 60.3 %all-gather.8.cloned.1.call-start = ((), (), s32[]{:S(2)}) async-start(), calls=%async_computation.2 | async-start | bytes 10616832 | tf_op jit(solution)/shard_map/all_gather | solution.py:25
  7.9 184.4 %all-gather.6.cloned.1.call-start = ((), (), s32[]{:S(2)}) async-start(), calls=%async_computation.1 | async-start | bytes 20054016 | tf_op jit(solution)/shard_map/all_gather | solution.py:28
  11.2 305.1 %all-gather.12.cloned.1.call-start = ((), (), s32[]{:S(2)}) async-start(), calls=%async_computation.4 | async-start | bytes 20054016 | tf_op jit(solution)/shard_map/all_gather | solution.py:36
  11.9 360.6 %all-gather.10.cloned.1.call-start = ((), (), s32[]{:S(2)}) async-start(), calls=%async_computation.3 | async-start | bytes 10616832 | tf_op jit(solution)/shard_map/all_gather | solution.py:33
  226.4 317.1 %copy-start = (f32[768,384]{1,0:T(8,128)S(1)}, f32[768,384]{1,0:T(8,128)}, u32[]{:S(2)}) copy-start(f32[768,384]{1,0:T(8,128)} %fusion.5) | copy-start | bytes 3538948
  226.4 317.0 %all-gather.14.cloned.1.call-start = ((), (), s32[]{:S(2)}) async-start(), calls=%async_computation.5 | async-start | bytes 20054016 | tf_op jit(solution)/shard_map/all_gather | solution.py:42
  421.3 212.8 %reduce-scatter.2.cloned.1.call-start = ((), (), s32[]{:S(2)}) async-start(), calls=%async_computation.6 | async-start | bytes 10616832 | tf_op jit(solution)/shard_map/reduce_scatter | solution.py:43
  577.5 1.3 copy-start.1
  577.5 56.7 %copy-start.2 = (f32[768,384]{1,0:T(8,128)S(1)}, f32[768,384]{1,0:T(8,128)}, u32[]{:S(2)}) copy-start(f32[768,384]{1,0:T(8,128)} %param.8) | copy-start | bytes 3538948
Sparse Core Ops, SparseCore 0:
  9.7 57.7 all-gather.7
  70.3 121.9 all-gather.5
  194.5 121.7 all-gather.11
  318.4 54.1 all-gather.9
  421.5 121.9 all-gather.13
  577.6 56.4 reduce-scatter.1
where the time goes:
time: 644 us; the launch traced here: 643 us
  waiting for transfers between devices  504 us (78%)
  matrix products  117 us (18%)
  between operations  14.1 us (2%)
    all_gather x1, waiting for transfers between devices, per_device(): lax.all_gather(masked, 'col', axis=1, tiled=True)  125 us
    all_gather x1, waiting for transfers between devices, per_device(): gathered = lax.all_gather(sigma_cross, 'col', axis=1, tiled=True)  122 us
    all_gather x1, waiting for transfers between devices, per_device(): lax.all_gather(sigma_top, 'col', axis=1, tiled=True)  89.7 us
    all_gather x1, waiting for transfers between devices, per_device(): update_strip = lax.all_gather(update, 'row', axis=0, tiled=True)  56.3 us
    all_gather x1, waiting for transfers between devices, per_device(): inverse_strip = lax.all_gather(factor_inverse, 'row', axis=0, tiled=True)  55.5 us
    reduce_scatter x1, waiting for transfers between devices, per_device(): lax.psum_scatter(transposed_rows(gathered, update), 'row', scatter_dimens...  54 us
    dot_general x1, matrix products, per_device(): jnp.dot(lax.all_gather(sigma_top, 'col', axis=1, tiled=True), rows_used,...  48.7 us
    dot_general x1, matrix products, per_device(): jnp.dot(lax.all_gather(masked, 'col', axis=1, tiled=True), rows_used, pre...  34.1 us
  transfers between devices with their start and end apart: 6, of which 6 were waited for; matrix products, arithmetic and copies ran while one was open for 6% of the time, Pallas kernels for 0%

commit v1 on v0

--- a/solution.py
+++ b/solution.py
@@ -33,7 +33,9 @@
     update_strip = lax.all_gather(update, "row", axis=0, tiled=True)
     rows_used = update_strip
     product = jnp.dot(
-        lax.all_gather(sigma_top, "col", axis=1, tiled=True),
+        jnp.concatenate(
+            lax.all_to_all(jnp.stack([sigma_top] * lax.axis_size("col")), "col", 0, 0), axis=1
+        ),
         rows_used,
         precision=lax.Precision.HIGHEST,
         preferred_element_type=jnp.float32,

time: 644 us -> 739 us (1.15)
  waiting for transfers between devices: 504 us -> 601 us
  matrix products: 117 us -> 96.4 us
  local copies, waits for them, and re-layouts: 2.64 us -> 12.6 us
  starting transfers between devices: 0.64 us -> 9.49 us
    all_gather x1, waiting for transfers between devices: 125 us -> 321 us  [per_device(): lax.all_gather(masked, 'col', axis=1, tiled=True)]
    all_gather x1 -> x0, waiting for transfers between devices: 89.7 us -> none  [per_device(): lax.all_gather(sigma_top, 'col', axis=1, tiled=True)]
    dot_general x1, matrix products: 48.7 us -> 28.2 us  [per_device(): jnp.dot(jnp.concatenate(lax.all_to_all(jnp.stack([sigma_top] * lax.axis_s...]
    all_gather x1, waiting for transfers between devices: 55.5 us -> 37.4 us  [per_device(): inverse_strip = lax.all_gather(factor_inverse, 'row', axis=0, tiled=True)]
    all_gather x1, waiting for transfers between devices: 56.3 us -> 66.2 us  [per_device(): update_strip = lax.all_gather(update, 'row', axis=0, tiled=True)]
    all_to_all x0 -> x1, starting transfers between devices: none -> 8.89 us  [per_device(): lax.all_to_all(jnp.stack([sigma_top] * lax.axis_size('col')), 'col', 0, 0)]
    another operation x0 -> x1, local copies, waits for them, and re-layouts: none -> 8.3 us  [per_device(): jnp.stack([sigma_top] * lax.axis_size('col'))]
  transfers between devices with their start and end apart: 6 -> 6, of which waited for: 6 -> 5; matrix products, arithmetic and copies ran while one was open for 6% -> 7% of each run, Pallas kernels for 0% -> 0%
where the time goes in v1:
time: 739 us
  waiting for transfers between devices  601 us (81%)
  matrix products  96.4 us (13%)
  between operations  13.8 us (2%)
  local copies, waits for them, and re-layouts  12.6 us (2%)
  starting transfers between devices  9.49 us (1%)
    all_gather x1, waiting for transfers between devices, per_device(): lax.all_gather(masked, 'col', axis=1, tiled=True)  321 us
    all_gather x1, waiting for transfers between devices, per_device(): gathered = lax.all_gather(sigma_cross, 'col', axis=1, tiled=True)  122 us
    all_gather x1, waiting for transfers between devices, per_device(): update_strip = lax.all_gather(update, 'row', axis=0, tiled=True)  66.2 us
    reduce_scatter x1, waiting for transfers between devices, per_device(): lax.psum_scatter(transposed_rows(gathered, update), 'row', scatter_dimens...  54 us
    all_gather x1, waiting for transfers between devices, per_device(): inverse_strip = lax.all_gather(factor_inverse, 'row', axis=0, tiled=True)  37.4 us
    dot_general x1, matrix products, per_device(): jnp.dot(lax.all_gather(masked, 'col', axis=1, tiled=True), rows_used, pre...  34.1 us
    dot_general x1, matrix products, transposed_rows(): lax.dot_general(gathered, right_side, (((0,), (0,)), ((), ())), precision...  34 us
    dot_general x1, matrix products, per_device(): jnp.dot(jnp.concatenate(lax.all_to_all(jnp.stack([sigma_top] * lax.axis_s...  28.2 us
  transfers between devices with their start and end apart: 6, of which 5 were waited for; matrix products, arithmetic and copies ran while one was open for 7% of the time, Pallas kernels for 0%

profile of v1, /device:TPU:1, one launch (start us, length us, event | category | flops | bytes accessed | tf_op | source)
XLA Modules:
  0.0 739.1 jit_solution(17816218260355831227)
XLA Ops:
  7.2 0.0 all-gather.7.cloned.1.call-start
  7.2 0.7 all-gather.7.cloned.1.call-update
  7.9 0.0 all-gather.5.cloned.1.call-start
  8.0 0.7 compare_reduce_fusion
  8.7 2.5 broadcast_select_fusion
  11.2 0.0 all-gather.5.cloned.1.call-update
  11.2 1.6 copy.10
  12.8 8.3 %stack.2 = f32[16,768,384]{1,2,0:T(8,128)} broadcast(f32[768,384]{0,1:T(8,128)S(1)} %copy.10), dimensions={1,2} | broadcast | bytes 20054016 | tf_op jit(solution)/shard_map/stack | solution.py:37
  21.1 8.9 %all-to-all-start = ((f32[16,768,384]{1,2,0:T(8,128)}), f32[16,768,384]{1,2,0:T(8,128)}, u32[]{:S(2)}, u32[]{:S(2)}) async-start(f32[16,768,384]{1,2,0:T(8,128)} %stack.2), calls=%async_computation | async-start | bytes 37748736 | tf_op jit(solution)/shard_map/all_to_all | solution.py:37
  30.0 0.0 all-gather.9.cloned.1.call-start
  30.1 37.4 %all-gather.7.cloned.1.call-done = f32[6144,384]{1,0:T(8,128)} async-done(((f32[768,384]{1,0:T(8,128)}), f32[6144,384]{1,0:T(8,128)}) %all-gather.7.cloned.1.call-update) | async-done | bytes 9437200 | tf_op jit(solution)/shard_map/all_gather | solution.py:25
  67.5 321.1 %all-gather.5.cloned.1.call-done = f32[768,6144]{1,0:T(8,128)} async-done(((f32[768,384]{1,0:T(8,128)}), f32[768,6144]{1,0:T(8,128)}) %all-gather.5.cloned.1.call-update) | async-done | bytes 18874384 | tf_op jit(solution)/shard_map/all_gather | solution.py:28
  388.6 34.1 %fusion.5 = f32[768,384]{1,0:T(8,128)} fusion(f32[768,6144]{1,0:T(8,128)} %all-gather.5.cloned.1.call-done, f32[6144,384]{1,0:T(8,128)} %all-gather.7.cloned.1.call-done), kind=kOutput, calls=%fused_computation.14 | convolution fusion | flops 21743271936 | bytes 29491200 | tf_op jit(solution)/shard_map/dot_general | solution.py:27
  422.7 0.0 all-gather.9.cloned.1.call-update
  422.7 0.2 all-gather.11.cloned.1.call-start
  422.9 0.0 all-to-all-done
  423.0 66.2 %all-gather.9.cloned.1.call-done = f32[6144,384]{1,0:T(8,128)} async-done(((f32[768,384]{1,0:T(8,128)}), f32[6144,384]{1,0:T(8,128)}) %all-gather.9.cloned.1.call-update) | async-done | bytes 9437200 | tf_op jit(solution)/shard_map/all_gather | solution.py:33
  489.1 0.0 copy-start
  489.1 28.2 %fusion.1 = f32[768,384]{0,1:T(8,128)} fusion(f32[6144,384]{1,0:T(8,128)} %all-gather.9.cloned.1.call-done, f32[768,6144]{0,1:T(8,128)} %bitcast.1, pred[768]{0:T(1024)(128)(4,1)S(1)} %compare_reduce_fusion), kind=kOutput, calls=%fused_computation.2 | convolution fusion | flops 21743861760 | bytes 29491968 | tf_op jit(solution)/shard_map/dot_general | solution.py:35
  517.4 0.0 all-gather.11.cloned.1.call-update
  517.4 0.3 reduce-scatter.2.cloned.1.call-start
  517.7 121.8 %all-gather.11.cloned.1.call-done = f32[768,6144]{0,1:T(8,128)} async-done(((f32[768,384]{0,1:T(8,128)}), f32[768,6144]{0,1:T(8,128)}) %all-gather.11.cloned.1.call-update) | async-done | bytes 18874384 | tf_op jit(solution)/shard_map/all_gather | solution.py:44
  639.5 0.0 copy-done
  639.5 34.0 %fusion.6 = f32[6144,384]{1,0:T(8,128)} fusion(f32[768,6144]{0,1:T(8,128)} %all-gather.11.cloned.1.call-done, f32[768,384]{1,0:T(8,128)S(1)} %copy-done), kind=kOutput, calls=%fused_computation.15 | convolution fusion | flops 21743271936 | bytes 29491200 | tf_op jit(solution)/shard_map/dot_general | solution.py:10
  673.5 0.0 copy-start.1
  673.5 0.0 copy-start.2
  673.5 0.0 reduce-scatter.2.cloned.1.call-update
  673.6 1.2 copy-done.1
  674.8 1.4 copy.11
  676.2 54.0 %reduce-scatter.2.cloned.1.call-done = f32[768,384]{1,0:T(8,128)} async-done(((f32[6144,384]{1,0:T(8,128)}), f32[768,384]{1,0:T(8,128)}) %reduce-scatter.2.cloned.1.call-update) | async-done | bytes 1179664 | tf_op jit(solution)/shard_map/reduce_scatter | solution.py:45
  730.2 0.0 copy-done.2
  730.2 2.4 sub.10
  (1 shorter events, 0.0 us)
Async XLA Ops:
  7.2 60.3 %all-gather.7.cloned.1.call-start = ((), (), s32[]{:S(2)}) async-start(), calls=%async_computation.3 | async-start | bytes 10616832 | tf_op jit(solution)/shard_map/all_gather | solution.py:25
  7.9 380.7 %all-gather.5.cloned.1.call-start = ((), (), s32[]{:S(2)}) async-start(), calls=%async_computation.2 | async-start | bytes 20054016 | tf_op jit(solution)/shard_map/all_gather | solution.py:28
  21.1 401.8 %all-to-all-start = ((f32[16,768,384]{1,2,0:T(8,128)}), f32[16,768,384]{1,2,0:T(8,128)}, u32[]{:S(2)}, u32[]{:S(2)}) async-start(f32[16,768,384]{1,2,0:T(8,128)} %stack.2), calls=%async_computation | async-start | bytes 37748736 | tf_op jit(solution)/shard_map/all_to_all | solution.py:37
  30.0 459.1 %all-gather.9.cloned.1.call-start = ((), (), s32[]{:S(2)}) async-start(), calls=%async_computation.4 | async-start | bytes 10616832 | tf_op jit(solution)/shard_map/all_gather | solution.py:33
  422.7 216.8 %all-gather.11.cloned.1.call-start = ((), (), s32[]{:S(2)}) async-start(), calls=%async_computation.5 | async-start | bytes 20054016 | tf_op jit(solution)/shard_map/all_gather | solution.py:44
  489.1 150.4 %copy-start = (f32[768,384]{1,0:T(8,128)S(1)}, f32[768,384]{1,0:T(8,128)}, u32[]{:S(2)}) copy-start(f32[768,384]{1,0:T(8,128)} %fusion.5) | copy-start | bytes 3538948
  517.4 212.8 %reduce-scatter.2.cloned.1.call-start = ((), (), s32[]{:S(2)}) async-start(), calls=%async_computation.6 | async-start | bytes 10616832 | tf_op jit(solution)/shard_map/reduce_scatter | solution.py:45
  673.5 1.3 copy-start.1
  673.5 56.7 %copy-start.2 = (f32[768,384]{1,0:T(8,128)S(1)}, f32[768,384]{1,0:T(8,128)}, u32[]{:S(2)}) copy-start(f32[768,384]{1,0:T(8,128)} %param.8) | copy-start | bytes 3538948
Sparse Core Ops, SparseCore 0:
  9.7 57.7 all-gather.6
  70.3 318.3 all-gather.4
  422.8 66.2 all-gather.8
  517.5 121.9 all-gather.10
  673.7 56.4 reduce-scatter.1
